TPU v7x, 32 devices: a whole 2x2x4 slice. The times are simulated.
32 devices in a mesh: segment: 16 (over z, y, core), rows: 2 (over x).
Axes of the slice: x: 2, y: 2, z: 4, core: 2. Of those that a mesh axis runs over, the one named last changes fastest.
Arguments:
- encoder_weight: bfloat16 [16, 3, 3, 384, 384], P('segment', None, None, 'rows'), may hold values from -0.109375 to 0.109375
- encoder_bias: float32 [16, 384], P('segment'), may hold values from -3 to 3
- decoder_weight: bfloat16 [16, 3, 3, 768, 384], P('segment', None, None, 'rows'), may hold values from -0.078125 to 0.078125
- decoder_bias: float32 [16, 384], P('segment'), may hold values from -3 to 3
- encoder_inputs: bfloat16 [16, 1, 6, 64, 384], P('segment', None, 'rows'), may hold values from -6 to 6
- decoder_inputs: bfloat16 [16, 1, 6, 64, 384], P('segment', None, 'rows'), may hold values from -6 to 6
- arrivals: bfloat16 [3, 1, 6, 64, 384], P(None, None, 'rows'), may hold values from -6 to 6
- skip_buffer: bfloat16 [16, 4, 1, 6, 64, 384], P('segment', None, None, 'rows'), may hold values from -6 to 6
Outputs:
- encoder_results: bfloat16 [16, 4, 1, 6, 64, 384], P('segment', None, None, 'rows')
- decoder_results: bfloat16 [16, 4, 1, 6, 64, 384], P('segment', None, None, 'rows')
All inputs are finite; a program needn't handle non-finite values.
Results may differ from a plain program's by a relative error of at most 0.0036.
Values may be sent and summed in bfloat16 or wider, within the bound.
A program may use at most 64 MiB of HBM per device.

v0:
```python
import jax
import jax.numpy as jnp
from jax import lax
from jax.sharding import PartitionSpec as P

NUMBERS = ("NHWC", "HWIO", "NHWC")


def padded(value, sides, width):
    for axis, dim in sides:
        peers, length = (lax.axis_size(axis), value.shape[dim])
        up = [(i, (i + 1) % peers) for i in range(peers - 1)]
        down = [(j, i) for i, j in up]
        last = lax.slice_in_dim(value, length - width, length, axis=dim)
        initial = lax.slice_in_dim(value, 0, width, axis=dim)
        before = lax.ppermute(last, axis, up)
        after = lax.ppermute(initial, axis, down)
        value = jnp.concatenate([before, value, after], axis=dim)
    return value


def shifted(block, axis, distance):
    devices = range(lax.axis_size(axis))
    route = [(i - distance, i) for i in devices if i - distance in devices]
    return lax.ppermute(block, axis, route)


def channel_part(source, kernel):
    return lax.conv_general_dilated(
        source,
        kernel,
        (1, 1),
        ((0, 0), (1, 1)),
        dimension_numbers=NUMBERS,
        preferred_element_type=jnp.float32,
    )


def finish(result, offset, rim_after, first_row, total_rows):
    result = jax.nn.silu(result + offset)
    if rim_after > 0:
        global_row = first_row - rim_after + jnp.arange(result.shape[1])
        inside = (global_row >= 0) & (global_row < total_rows)
        result = jnp.where(inside[None, :, None, None], result, 0.0)
    return result.astype(jnp.bfloat16)


def trim_rows(source, have_rim, want_rim):
    excess = have_rim - want_rim
    if excess == 0:
        return source
    return source[:, excess : source.shape[1] - excess]


def shards(
    encoder_weight,
    encoder_bias,
    decoder_weight,
    decoder_bias,
    encoder_inputs,
    decoder_inputs,
    arrivals,
    skip_buffer,
):
    segment_count = lax.axis_size("segment")
    segment_index = lax.axis_index("segment")
    rows_local = encoder_inputs.shape[2]
    total_rows = rows_local * lax.axis_size("rows")
    first_row = lax.axis_index("rows") * rows_local
    channels = encoder_weight.shape[4]
    tick_count = skip_buffer.shape[1]
    skip_lag = 2 * (segment_count - segment_index) - 1
    margin = 2
    paired = decoder_weight.reshape(1, 3, 3, decoder_weight.shape[3] // 2, 2 * channels)
    encoder_offset = encoder_bias[0]
    decoder_offset = decoder_bias[0]
    kernels = [None, None]
    gathered = (
        lax.all_gather(encoder_weight, "rows", axis=3, tiled=True),
        lax.all_gather(paired, "rows", axis=3, tiled=True),
    )
    kernels[0] = gathered[0][0]
    kernels[1] = gathered[1].reshape(3, 3, 2 * channels, channels)
    encoder_now = encoder_inputs[0]
    decoder_now = decoder_inputs[0]
    arrival_state = [(arrivals[number], 0) for number in range(tick_count - 1)]
    skip_state = [(skip_buffer[0, number], 0) for number in range(tick_count)]
    encoder_made = []
    encoder_cores = []
    decoder_cores = []

    def pick_skip(period, want_rim):
        base_skip, base_rim = skip_state[period]
        chosen = trim_rows(base_skip, base_rim, want_rim)
        for earlier in range(period):
            if (period - earlier) % 2 == 1:
                made_value, made_rim = encoder_made[earlier]
                chosen = jnp.where(
                    skip_lag == period - earlier, trim_rows(made_value, made_rim, want_rim), chosen
                )
        return chosen

    for period in range(tick_count):
        position = period % margin
        rim_before = margin - position
        if position == 0:
            skip_now = pick_skip(period, 0)
            pieces = [encoder_now, decoder_now, skip_now]
            pieces = pieces + [arrival_state[period][0], skip_state[period + 1][0]]
            joined = jnp.concatenate(pieces, axis=3)
            rimmed = padded(joined, (("rows", 1),), margin)
            sections = [
                rimmed[..., number * channels : (number + 1) * channels]
                for number in range(len(pieces))
            ]
            encoder_now = sections[0]
            decoder_now = sections[1]
            skip_now = sections[2]
            arrival_state[period] = (sections[3], margin)
            skip_state[period + 1] = (sections[4], margin)
        else:
            skip_now = pick_skip(period, rim_before)
        rim_after = rim_before - 1
        decoder_source = jnp.concatenate([decoder_now, skip_now], axis=3)
        encoder_out = finish(
            channel_part(encoder_now, kernels[0]), encoder_offset, rim_after, first_row, total_rows
        )
        decoder_out = finish(
            channel_part(decoder_source, kernels[1]),
            decoder_offset,
            rim_after,
            first_row,
            total_rows,
        )
        encoder_made.append((encoder_out, rim_after))
        encoder_cores.append(trim_rows(encoder_out, rim_after, 0))
        decoder_cores.append(trim_rows(decoder_out, rim_after, 0))
        if period + 1 < tick_count:
            encoder_moved = shifted(encoder_out, "segment", 1)
            decoder_moved = shifted(decoder_out, "segment", -1)
            arrival, arrival_rim = arrival_state[period]
            encoder_now = jnp.where(
                segment_index == 0, trim_rows(arrival, arrival_rim, rim_after), encoder_moved
            )
            decoder_now = jnp.where(segment_index == segment_count - 1, encoder_out, decoder_moved)
    return (jnp.stack(encoder_cores, axis=0)[None], jnp.stack(decoder_cores, axis=0)[None])


def solution(mesh):
    return jax.shard_map(
        shards,
        mesh=mesh,
        in_specs=(
            P("segment", None, None, "rows", None),
            P("segment", None),
            P("segment", None, None, "rows", None),
            P("segment", None),
            P("segment", None, "rows", None, None),
            P("segment", None, "rows", None, None),
            P(None, None, "rows", None, None),
            P("segment", None, None, "rows", None, None),
        ),
        out_specs=(
            P("segment", None, None, "rows", None, None),
            P("segment", None, None, "rows", None, None),
        ),
        check_vma=False,
    )
```

profile of v0, /device:TPU:7, one launch (start us, length us, event | category | flops | bytes accessed | tf_op | source)
XLA Modules:
  0.0 226.2 jit_solution(11212212457153941616)
XLA Ops:
  7.2 0.7 all-gather.3.cloned.1.call-update
  7.9 5.1 %reshape.31 = bf16[1,3,3,192,768]{4,3,2,1,0:T(8,128)(2,1)} reshape(bf16[1,3,3,384,384]{4,3,2,1,0:T(8,128)(2,1)} %param.10) | data formatting | bytes 5308416 | tf_op jit(solution)/shard_map/reshape | solution.py:74
  13.1 0.9 copy-done.6
  14.3 0.8 fusion.160
  15.3 0.8 fusion.161
  16.3 0.7 fusion.159
  17.0 2.2 collective-permute-start.1
  19.2 1.3 collective-permute-start
  20.6 19.6 %collective-permute-done.1 = bf16[1,2,64,1920]{3,1,2,0:T(2,128)(2,1)S(1)} collective-permute-done((bf16[1,2,64,1920]{3,1,2,0:T(2,128)(2,1)S(1)}, bf16[1,2,64,1920]{3,1,2,0:T(2,128)(2,1)S(1)}, u32[]{:S(2)}, u32[]{:S(2)}) %collective-permute-start.1) | collective-permute-done | bytes 491552 | tf_op jit(solution)/shard_map/ppermute | solution.py:17
  40.2 4.3 %collective-permute-done = bf16[1,2,64,1920]{3,1,2,0:T(2,128)(2,1)S(1)} collective-permute-done((bf16[1,2,64,1920]{3,1,2,0:T(2,128)(2,1)S(1)}, bf16[1,2,64,1920]{3,1,2,0:T(2,128)(2,1)S(1)}, u32[]{:S(2)}, u32[]{:S(2)}) %collective-permute-start) | collective-permute-done | bytes 491552 | tf_op jit(solution)/shard_map/ppermute | solution.py:16
  45.0 0.6 maximum_bitcast_fusion.1
  46.0 0.7 slice.130
  46.7 13.1 %all-gather.3.cloned.1.call-done = bf16[1,3,3,384,384]{4,3,2,1,0:T(8,128)(2,1)} async-done(((bf16[1,3,3,192,384]{4,3,2,1,0:T(8,128)(2,1)}), bf16[1,3,3,384,384]{4,3,2,1,0:T(8,128)(2,1)}) %all-gather.3.cloned.1.call-update) | async-done | bytes 2654224 | tf_op jit(solution)/shard_map/all_gather | solution.py:79
  59.8 4.0 %select_convert_fusion.3 = bf16[5,8,9,384]{3,1,2,0:T(8,128)(2,1)} fusion(bf16[1,3,3,384,384]{4,3,2,1,0:T(8,128)(2,1)} %all-gather.3.cloned.1.call-done, bf16[7,1,7,2,384]{4,2,3,0,1:T(8,128)(2,1)S(1)} %slice.124, bf16[7,1,8,9,384]{4,2,3,0,1:T(8,128)(2,1)S(1)} %copy.16, f32[384]{0:T(512)S(1)} %reduce, pred[5]{0:T(512)(128)(4,1)S(1)} %compare_and_fusion, ...), kind=kOutput, calls=%fused_computation.65 | convolution fusion | flops 958040064 | bytes 3394637 | tf_op jit(solution)/shard_map/conv_general_dilated | solution.py:29
  63.8 1.0 copy.57
  64.8 0.8 slice_bitcast_fusion.3
  65.6 3.7 %collective-permute-start.2 = (bf16[1,5,64,384]{3,1,2,0:T(8,128)(2,1)}, bf16[1,5,64,384]{3,1,2,0:T(8,128)(2,1)}, u32[]{:S(2)}, u32[]{:S(2)}) collective-permute-start(bf16[1,5,64,384]{3,1,2,0:T(8,128)(2,1)} %slice_bitcast_fusion.3), channel_id=1, source_target_pairs={{0,2},{2,4},{4,6},{6,8},{8,10},{10,12},{12,14},{14,16},{16,18},{18... | collective-permute-start | bytes 737288 | tf_op jit(solution)/shard_map/ppermute | solution.py:25
  69.3 61.4 %all-gather.5.cloned.1.call-done = bf16[1,3,3,384,768]{4,3,2,1,0:T(8,128)(2,1)} async-done(((bf16[1,3,3,192,768]{4,3,2,1,0:T(8,128)(2,1)}), bf16[1,3,3,384,768]{4,3,2,1,0:T(8,128)(2,1)}) %all-gather.5.cloned.1.call-update) | async-done | bytes 5308432 | tf_op jit(solution)/shard_map/all_gather | solution.py:80
  130.7 8.7 %reshape.32 = bf16[3,3,768,384]{3,2,1,0:T(8,128)(2,1)} reshape(bf16[1,3,3,384,768]{4,3,2,1,0:T(8,128)(2,1)} %all-gather.5.cloned.1.call-done) | data formatting | bytes 10616832 | tf_op jit(solution)/shard_map/reshape | solution.py:83
  139.3 5.4 %select_convert_fusion.2 = bf16[5,8,9,384]{3,1,2,0:T(8,128)(2,1)S(1)} fusion(bf16[3,3,768,384]{3,2,1,0:T(8,128)(2,1)} %reshape.32, bf16[7,1,7,2,768]{4,2,3,0,1:T(8,128)(2,1)} %slice.130, bf16[7,1,8,9,768]{4,2,3,0,1:T(8,128)(2,1)S(1)} %copy.26, f32[384]{0:T(512)S(1)} %reduce.1, pred[5]{0:T(512)(128)(4,1)S(1)} %compare_and_fusion, pred[8,9]{0,1:T(8,128)(4,1)S(1)} %copy-done.12), kind=kOutput, calls=%fused_computation.64 | convolution fusion | flops 1914974208 | bytes 6511181 | tf_op jit(solution)/shard_map/conv_general_dilated | solution.py:29
  144.8 0.8 slice_bitcast_fusion.2
  145.6 2.6 %collective-permute-start.4 = (bf16[1,5,64,384]{3,1,2,0:T(8,128)(2,1)}, bf16[1,5,64,384]{3,1,2,0:T(8,128)(2,1)S(1)}, u32[]{:S(2)}, u32[]{:S(2)}) collective-permute-start(bf16[1,5,64,384]{3,1,2,0:T(8,128)(2,1)} %slice_bitcast_fusion.2), channel_id=1, source_target_pairs={{2,0},{4,2},{6,4},{8,6},{10,8},{12,10},{14,12},{16,14},{18,16},{20... | collective-permute-start | bytes 737288 | tf_op jit(solution)/shard_map/ppermute | solution.py:25
  148.2 7.6 %collective-permute-done.4 = bf16[1,5,64,384]{3,1,2,0:T(8,128)(2,1)S(1)} collective-permute-done((bf16[1,5,64,384]{3,1,2,0:T(8,128)(2,1)}, bf16[1,5,64,384]{3,1,2,0:T(8,128)(2,1)S(1)}, u32[]{:S(2)}, u32[]{:S(2)}) %collective-permute-start.4) | collective-permute-done | bytes 245792 | tf_op jit(solution)/shard_map/ppermute | solution.py:25
  155.8 1.9 fusion.93
  157.9 1.0 multiply_convert_fusion.3
  159.2 2.2 collective-permute-start.3
  161.9 1.8 multiply_convert_fusion.2
  163.9 2.4 %collective-permute-start.5 = (bf16[1,3,64,384]{3,1,2,0:T(4,128)(2,1)S(1)}, bf16[1,3,64,384]{3,1,2,0:T(4,128)(2,1)S(1)}, u32[]{:S(2)}, u32[]{:S(2)}) collective-permute-start(bf16[1,3,64,384]{3,1,2,0:T(4,128)(2,1)S(1)} %get-tuple-element.22), channel_id=1, source_target_pairs={{2,0},{4,2},{6,4},{8,6},{10,8},{12,10},{14,12},{16,14},{18,16},{20... | collective-permute-start | bytes 442376 | tf_op jit(solution)/shard_map/ppermute | solution.py:25
  166.5 5.3 %collective-permute-done.5 = bf16[1,3,64,384]{3,1,2,0:T(4,128)(2,1)S(1)} collective-permute-done((bf16[1,3,64,384]{3,1,2,0:T(4,128)(2,1)S(1)}, bf16[1,3,64,384]{3,1,2,0:T(4,128)(2,1)S(1)}, u32[]{:S(2)}, u32[]{:S(2)}) %collective-permute-start.5) | collective-permute-done | bytes 147488 | tf_op jit(solution)/shard_map/ppermute | solution.py:25
  172.5 1.6 fusion.158
  174.1 3.1 %collective-permute-start.7 = (bf16[1,2,64,1920]{3,1,2,0:T(2,128)(2,1)}, bf16[1,2,64,1920]{3,1,2,0:T(2,128)(2,1)S(1)}, u32[]{:S(2)}, u32[]{:S(2)}) collective-permute-start(bf16[1,2,64,1920]{3,1,2,0:T(2,128)(2,1)} %get-tuple-element.9), channel_id=1, source_target_pairs={{1,0},{3,2},{5,4},{7,6},{9,8},{11,10},{13,12},{15,14},{17,16},{19,... | collective-permute-start | bytes 1474568 | tf_op jit(solution)/shard_map/ppermute | solution.py:17
  177.3 1.3 collective-permute-start.6
  178.6 1.6 slice.125
  180.1 1.0 copy.17
  181.2 5.6 %collective-permute-done.7 = bf16[1,2,64,1920]{3,1,2,0:T(2,128)(2,1)S(1)} collective-permute-done((bf16[1,2,64,1920]{3,1,2,0:T(2,128)(2,1)}, bf16[1,2,64,1920]{3,1,2,0:T(2,128)(2,1)S(1)}, u32[]{:S(2)}, u32[]{:S(2)}) %collective-permute-start.7) | collective-permute-done | bytes 491552 | tf_op jit(solution)/shard_map/ppermute | solution.py:17
  186.7 4.0 %collective-permute-done.6 = bf16[1,2,64,1920]{3,1,2,0:T(2,128)(2,1)S(1)} collective-permute-done((bf16[1,2,64,1920]{3,1,2,0:T(2,128)(2,1)}, bf16[1,2,64,1920]{3,1,2,0:T(2,128)(2,1)S(1)}, u32[]{:S(2)}, u32[]{:S(2)}) %collective-permute-start.6) | collective-permute-done | bytes 491552 | tf_op jit(solution)/shard_map/ppermute | solution.py:16
  191.3 1.6 select_convert_fusion.1
  193.0 4.2 %collective-permute-start.8 = (bf16[1,5,64,384]{3,1,2,0:T(8,128)(2,1)S(1)}, bf16[1,5,64,384]{3,1,2,0:T(8,128)(2,1)S(1)}, u32[]{:S(2)}, u32[]{:S(2)}) collective-permute-start(bf16[1,5,64,384]{3,1,2,0:T(8,128)(2,1)S(1)} %slice_bitcast_fusion.1), channel_id=1, source_target_pairs={{0,2},{2,4},{4,6},{6,8},{8,10},{10,12},{12,14},{14,16},{16,18},{18... | collective-permute-start | bytes 737288 | tf_op jit(solution)/shard_map/ppermute | solution.py:25
  198.2 2.9 %select_convert_fusion = bf16[5,8,9,384]{3,1,2,0:T(8,128)(2,1)S(1)} fusion(bf16[3,3,768,384]{3,2,1,0:T(8,128)(2,1)S(1)} %bitcast.201, bf16[7,1,7,2,768]{4,2,3,0,1:T(8,128)(2,1)S(1)} %slice.144, bf16[7,1,8,9,768]{4,2,3,0,1:T(8,128)(2,1)S(1)} %copy.47, f32[384]{0:T(512)S(1)} %reduce.1, pred[5]{0:T(512)(128)(4,1)S(1)} %compare_and_fusion, ...), kind=kOutput, calls=%fused_computation.62 | convolution fusion | flops 1914974208 | bytes 6511181 | tf_op jit(solution)/shard_map/conv_general_dilated | solution.py:29
  201.2 2.1 collective-permute-start.9
  203.9 7.3 %collective-permute-done.9 = bf16[1,5,64,384]{3,1,2,0:T(8,128)(2,1)S(1)} collective-permute-done((bf16[1,5,64,384]{3,1,2,0:T(8,128)(2,1)S(1)}, bf16[1,5,64,384]{3,1,2,0:T(8,128)(2,1)S(1)}, u32[]{:S(2)}, u32[]{:S(2)}) %collective-permute-start.9) | collective-permute-done | bytes 245792 | tf_op jit(solution)/shard_map/ppermute | solution.py:25
  211.2 1.0 fusion.91
  212.4 1.0 multiply_convert_fusion.1
  213.6 0.7 maximum_bitcast_fusion.3
  214.4 0.9 copy.55
  215.7 1.8 multiply_convert_fusion
  217.8 0.7 maximum_bitcast_fusion.5
  218.5 0.9 copy.56
  (103 shorter events, 6.6 us)
Async XLA Ops:
  7.2 52.6 %all-gather.3.cloned.1.call-start = ((), (), s32[]{:S(2)}) async-start(), calls=%async_computation | async-start | bytes 3981312 | tf_op jit(solution)/shard_map/all_gather | solution.py:79
  7.9 122.8 %all-gather.5.cloned.1.call-start = ((), (), s32[]{:S(2)}) async-start(), calls=%async_computation.1 | async-start | bytes 7962624 | tf_op jit(solution)/shard_map/all_gather | solution.py:80
  13.1 0.9 copy-start.6
  13.1 1.0 copy-start.7
  13.1 1.2 copy-start.3
  13.1 2.2 copy-start.5
  15.1 5.5 %copy-start.8 = (f32[1,384]{1,0:T(1,128)S(1)}, f32[1,384]{1,0:T(1,128)}, u32[]{:S(2)}) copy-start(f32[1,384]{1,0:T(1,128)} %param.9) | copy-start | bytes 4612
  15.1 5.5 %copy-start.9 = (f32[1,384]{1,0:T(1,128)S(1)}, f32[1,384]{1,0:T(1,128)}, u32[]{:S(2)}) copy-start(f32[1,384]{1,0:T(1,128)} %param.11) | copy-start | bytes 4612
  17.0 23.2 %collective-permute-start.1 = (bf16[1,2,64,1920]{3,1,2,0:T(2,128)(2,1)S(1)}, bf16[1,2,64,1920]{3,1,2,0:T(2,128)(2,1)S(1)}, u32[]{:S(2)}, u32[]{:S(2)}) collective-permute-start(bf16[1,2,64,1920]{3,1,2,0:T(2,128)(2,1)S(1)} %get-tuple-element.11), channel_id=1, source_target_pairs={{1,0},{3,2},{5,4},{7,6},{9,8},{11,10},{13,12},{15,14},{17,16},{19,... | collective-permute-start | bytes 1474568 | tf_op jit(solution)/shard_map/ppermute | solution.py:17
  19.2 25.3 %collective-permute-start = (bf16[1,2,64,1920]{3,1,2,0:T(2,128)(2,1)S(1)}, bf16[1,2,64,1920]{3,1,2,0:T(2,128)(2,1)S(1)}, u32[]{:S(2)}, u32[]{:S(2)}) collective-permute-start(bf16[1,2,64,1920]{3,1,2,0:T(2,128)(2,1)S(1)} %get-tuple-element.10), channel_id=1, source_target_pairs={{0,1},{2,3},{4,5},{6,7},{8,9},{10,11},{12,13},{14,15},{16,17},{18,... | collective-permute-start | bytes 1474568 | tf_op jit(solution)/shard_map/ppermute | solution.py:16
  45.7 14.1 %copy-start.12 = (pred[8,9]{0,1:T(8,128)(4,1)S(1)}, pred[8,9]{0,1:T(8,128)(4,1)}, u32[]{:S(2)}) copy-start(pred[8,9]{0,1:T(8,128)(4,1)} %constant.79) | copy-start | bytes 220
  65.6 82.6 %collective-permute-start.2 = (bf16[1,5,64,384]{3,1,2,0:T(8,128)(2,1)}, bf16[1,5,64,384]{3,1,2,0:T(8,128)(2,1)}, u32[]{:S(2)}, u32[]{:S(2)}) collective-permute-start(bf16[1,5,64,384]{3,1,2,0:T(8,128)(2,1)} %slice_bitcast_fusion.3), channel_id=1, source_target_pairs={{0,2},{2,4},{4,6},{6,8},{8,10},{10,12},{12,14},{14,16},{16,18},{18... | collective-permute-start | bytes 737288 | tf_op jit(solution)/shard_map/ppermute | solution.py:25
  145.6 10.2 %collective-permute-start.4 = (bf16[1,5,64,384]{3,1,2,0:T(8,128)(2,1)}, bf16[1,5,64,384]{3,1,2,0:T(8,128)(2,1)S(1)}, u32[]{:S(2)}, u32[]{:S(2)}) collective-permute-start(bf16[1,5,64,384]{3,1,2,0:T(8,128)(2,1)} %slice_bitcast_fusion.2), channel_id=1, source_target_pairs={{2,0},{4,2},{6,4},{8,6},{10,8},{12,10},{14,12},{16,14},{18,16},{20... | collective-permute-start | bytes 737288 | tf_op jit(solution)/shard_map/ppermute | solution.py:25
  148.2 9.7 %copy-start.10 = (bf16[1,3,3,384,384]{4,3,2,1,0:T(8,128)(2,1)S(1)}, bf16[1,3,3,384,384]{4,3,2,1,0:T(8,128)(2,1)}, u32[]{:S(2)}) copy-start(bf16[1,3,3,384,384]{4,3,2,1,0:T(8,128)(2,1)} %all-gather.3.cloned.1.call-done) | copy-start | bytes 7962628
  157.8 4.0 %slice-start = ((s8[5308416]{0:T(1024)(128)(4,1)}), s8[4194304]{0:T(1024)(128)(4,1)S(1)}, s32[]{:S(2)}) async-start(s8[5308416]{0:T(1024)(128)(4,1)} %bitcast.198), calls=%async_computation.2 | async-start | bytes 8388608
  157.9 3.9 %slice-start.1 = ((s8[5308416]{0:T(1024)(128)(4,1)}), s8[1114112]{0:T(1024)(128)(4,1)S(1)}, s32[]{:S(2)}) async-start(s8[5308416]{0:T(1024)(128)(4,1)} %bitcast.198), calls=%async_computation.3 | async-start | bytes 2228224
  159.2 7.2 %collective-permute-start.3 = (bf16[1,3,64,384]{3,1,2,0:T(4,128)(2,1)S(1)}, bf16[1,3,64,384]{3,1,2,0:T(4,128)(2,1)S(1)}, u32[]{:S(2)}, u32[]{:S(2)}) collective-permute-start(bf16[1,3,64,384]{3,1,2,0:T(4,128)(2,1)S(1)} %get-tuple-element.24), channel_id=1, source_target_pairs={{0,2},{2,4},{4,6},{6,8},{8,10},{10,12},{12,14},{14,16},{16,18},{18... | collective-permute-start | bytes 442376 | tf_op jit(solution)/shard_map/ppermute | solution.py:25
  161.9 4.5 %copy-start.2 = (bf16[1,1,3,64,384]{4,3,2,1,0:T(8,128)(2,1)S(1)}, bf16[1,1,3,64,384]{4,3,2,1,0:T(8,128)(2,1)}, u32[]{:S(2)}) copy-start(bf16[1,1,3,64,384]{4,3,2,1,0:T(8,128)(2,1)} %get-tuple-element.18) | copy-start | bytes 442372
  163.7 8.3 %copy-start = (bf16[1,1,1,3,64,384]{5,4,3,2,1,0:T(8,128)(2,1)S(1)}, bf16[1,1,1,3,64,384]{5,4,3,2,1,0:T(8,128)(2,1)}, u32[]{:S(2)}) copy-start(bf16[1,1,1,3,64,384]{5,4,3,2,1,0:T(8,128)(2,1)} %get-tuple-element.13) | copy-start | bytes 442372
  163.7 8.5 %copy-start.4 = (bf16[1,1,3,64,384]{4,3,2,1,0:T(8,128)(2,1)S(1)}, bf16[1,1,3,64,384]{4,3,2,1,0:T(8,128)(2,1)}, u32[]{:S(2)}) copy-start(bf16[1,1,3,64,384]{4,3,2,1,0:T(8,128)(2,1)} %get-tuple-element.17) | copy-start | bytes 442372
  163.7 8.6 %copy-start.1 = (bf16[1,1,1,3,64,384]{5,4,3,2,1,0:T(8,128)(2,1)S(1)}, bf16[1,1,1,3,64,384]{5,4,3,2,1,0:T(8,128)(2,1)}, u32[]{:S(2)}) copy-start(bf16[1,1,1,3,64,384]{5,4,3,2,1,0:T(8,128)(2,1)} %get-tuple-element.12) | copy-start | bytes 442372
  163.9 7.9 %collective-permute-start.5 = (bf16[1,3,64,384]{3,1,2,0:T(4,128)(2,1)S(1)}, bf16[1,3,64,384]{3,1,2,0:T(4,128)(2,1)S(1)}, u32[]{:S(2)}, u32[]{:S(2)}) collective-permute-start(bf16[1,3,64,384]{3,1,2,0:T(4,128)(2,1)S(1)} %get-tuple-element.22), channel_id=1, source_target_pairs={{2,0},{4,2},{6,4},{8,6},{10,8},{12,10},{14,12},{16,14},{18,16},{20... | collective-permute-start | bytes 442376 | tf_op jit(solution)/shard_map/ppermute | solution.py:25
  174.1 12.6 %collective-permute-start.7 = (bf16[1,2,64,1920]{3,1,2,0:T(2,128)(2,1)}, bf16[1,2,64,1920]{3,1,2,0:T(2,128)(2,1)S(1)}, u32[]{:S(2)}, u32[]{:S(2)}) collective-permute-start(bf16[1,2,64,1920]{3,1,2,0:T(2,128)(2,1)} %get-tuple-element.9), channel_id=1, source_target_pairs={{1,0},{3,2},{5,4},{7,6},{9,8},{11,10},{13,12},{15,14},{17,16},{19,... | collective-permute-start | bytes 1474568 | tf_op jit(solution)/shard_map/ppermute | solution.py:17
  177.3 13.5 %collective-permute-start.6 = (bf16[1,2,64,1920]{3,1,2,0:T(2,128)(2,1)}, bf16[1,2,64,1920]{3,1,2,0:T(2,128)(2,1)S(1)}, u32[]{:S(2)}, u32[]{:S(2)}) collective-permute-start(bf16[1,2,64,1920]{3,1,2,0:T(2,128)(2,1)} %get-tuple-element.8), channel_id=1, source_target_pairs={{0,1},{2,3},{4,5},{6,7},{8,9},{10,11},{12,13},{14,15},{16,17},{18,... | collective-permute-start | bytes 1474568 | tf_op jit(solution)/shard_map/ppermute | solution.py:16
  181.1 10.1 %copy-start.11 = (bf16[1,3,3,384,384]{4,3,2,1,0:T(8,128)(2,1)S(1)}, bf16[1,3,3,384,384]{4,3,2,1,0:T(8,128)(2,1)}, u32[]{:S(2)}) copy-start(bf16[1,3,3,384,384]{4,3,2,1,0:T(8,128)(2,1)} %all-gather.3.cloned.1.call-done) | copy-start | bytes 7962628
  191.2 7.0 %slice-start.2 = ((s8[5308416]{0:T(1024)(128)(4,1)}), s8[4194304]{0:T(1024)(128)(4,1)S(1)}, s32[]{:S(2)}) async-start(s8[5308416]{0:T(1024)(128)(4,1)} %bitcast.200), calls=%async_computation.4 | async-start | bytes 8388608
  191.3 6.9 %slice-start.3 = ((s8[5308416]{0:T(1024)(128)(4,1)}), s8[1114112]{0:T(1024)(128)(4,1)S(1)}, s32[]{:S(2)}) async-start(s8[5308416]{0:T(1024)(128)(4,1)} %bitcast.200), calls=%async_computation.5 | async-start | bytes 2228224
  193.0 10.9 %collective-permute-start.8 = (bf16[1,5,64,384]{3,1,2,0:T(8,128)(2,1)S(1)}, bf16[1,5,64,384]{3,1,2,0:T(8,128)(2,1)S(1)}, u32[]{:S(2)}, u32[]{:S(2)}) collective-permute-start(bf16[1,5,64,384]{3,1,2,0:T(8,128)(2,1)S(1)} %slice_bitcast_fusion.1), channel_id=1, source_target_pairs={{0,2},{2,4},{4,6},{6,8},{8,10},{10,12},{12,14},{14,16},{16,18},{18... | collective-permute-start | bytes 737288 | tf_op jit(solution)/shard_map/ppermute | solution.py:25
  201.2 10.0 %collective-permute-start.9 = (bf16[1,5,64,384]{3,1,2,0:T(8,128)(2,1)S(1)}, bf16[1,5,64,384]{3,1,2,0:T(8,128)(2,1)S(1)}, u32[]{:S(2)}, u32[]{:S(2)}) collective-permute-start(bf16[1,5,64,384]{3,1,2,0:T(8,128)(2,1)S(1)} %slice_bitcast_fusion), channel_id=1, source_target_pairs={{2,0},{4,2},{6,4},{8,6},{10,8},{12,10},{14,12},{16,14},{18,16},{20... | collective-permute-start | bytes 737288 | tf_op jit(solution)/shard_map/ppermute | solution.py:25
Sparse Core Ops, SparseCore 0:
  9.5 50.1 all-gather.2
  61.3 69.2 all-gather.4
where the time goes:
time: 227 us; the launch traced here: 226 us
  waiting for transfers between devices  129 us (57%)
  local copies, waits for them, and re-layouts  30.7 us (14%)
  starting transfers between devices  25.1 us (11%)
  matrix products  19.6 us (9%)
  between operations  14.9 us (7%)
  other arithmetic  7.07 us (3%)
    all_gather x1, waiting for transfers between devices, shards(): lax.all_gather(paired, 'rows', axis=3, tiled=True)  61.4 us
    ppermute x2, waiting for transfers between devices, padded(): after = lax.ppermute(initial, axis, down)  25.1 us
    ppermute x6, waiting for transfers between devices, shifted(): return lax.ppermute(block, axis, route)  20.2 us
    conv_general_dilated x8, matrix products, channel_part(): lax.conv_general_dilated(source, kernel, (1, 1), ((0, 0), (1, 1)), dimens...  19.6 us
    ppermute x6, starting transfers between devices, shifted(): return lax.ppermute(block, axis, route)  17.2 us
    all_gather x1, waiting for transfers between devices, shards(): lax.all_gather(encoder_weight, 'rows', axis=3, tiled=True)  13.1 us
    reshape x1, local copies, waits for them, and re-layouts, shards(): kernels[1] = gathered[1].reshape(3, 3, 2 * channels, channels)  8.7 us
    ppermute x2, waiting for transfers between devices, padded(): before = lax.ppermute(last, axis, up)  8.34 us
  transfers between devices with their start and end apart: 12, of which 9 were waited for; matrix products, arithmetic and copies ran while one was open for 18% of the time, Pallas kernels for 0%

commit v1 on v0

--- a/solution.py
+++ b/solution.py
@@ -1,6 +1,10 @@
+import functools
+
 import jax
 import jax.numpy as jnp
 from jax import lax
+from jax.experimental import pallas as pl
+from jax.experimental.pallas import tpu as pltpu
 from jax.sharding import PartitionSpec as P
 
 NUMBERS = ("NHWC", "HWIO", "NHWC")
@@ -52,7 +56,399 @@
     return source[:, excess : source.shape[1] - excess]
 
 
-def shards(
+MESH = pl.DeviceIdType.MESH
+SENT = jnp.bfloat16
+TOP = 32768.0
+
+
+def relay_kernel(
+    segments,
+    enc_w,
+    enc_b,
+    dec_w,
+    dec_b,
+    enc_in,
+    dec_in,
+    arrivals,
+    skips,
+    enc_out,
+    dec_out,
+    kernel,
+    skip_kernel,
+    held,
+    made,
+    skip_full,
+    partial,
+    scale,
+    columns,
+    total,
+    local_sem,
+    link_send,
+    link_recv,
+    relay_send,
+    relay_recv,
+):
+    s = lax.axis_index("segment")
+    r = lax.axis_index("rows")
+    ticks, half, width, channels = skips.shape
+    rows = 2 * half
+    cells = rows * width
+    taps = enc_w.shape[0]
+    part = enc_w.shape[2]
+    last = segments - 1
+    is_enc = r == 1
+    is_dec = r == 0
+
+    def link(number, src, dst):
+        return pltpu.make_async_remote_copy(
+            src_ref=src,
+            dst_ref=dst,
+            send_sem=link_send.at[number],
+            recv_sem=link_recv.at[number],
+            device_id={"segment": s, "rows": 1 - r},
+            device_id_type=MESH,
+        )
+
+    def relay(tick, segment, row):
+        return pltpu.make_async_remote_copy(
+            src_ref=made.at[tick],
+            dst_ref=held.at[tick + 1],
+            send_sem=relay_send.at[tick],
+            recv_sem=relay_recv.at[tick],
+            device_id={"segment": segment, "rows": row},
+            device_id_type=MESH,
+        )
+
+    def local(number, src, dst):
+        return pltpu.make_async_copy(src, dst, local_sem.at[number])
+
+    first, final = pl.ds(0, half), pl.ds(half, half)
+
+    skip_link = [link(t, skips.at[t], skip_full.at[t, first]) for t in range(ticks)]
+    base = ticks
+    input_link = link(base, enc_in, held.at[0, first])
+    weight_link = [
+        link(base + 1 + d, enc_w.at[d], kernel.at[d, :, pl.ds(0, part)]) for d in range(taps)
+    ]
+    base = base + 1 + taps
+    arrival_link = [
+        link(base + t, arrivals.at[t], held.at[t + 1, first]) for t in range(ticks - 1)
+    ]
+    base = base + ticks - 1
+    dec_link = [link(base + t, made.at[t, final], dec_out.at[t]) for t in range(ticks)]
+    back_input = link(0, dec_in, held.at[0, final])
+    partial_link = [link(1 + t, partial.at[t], partial.at[t]) for t in range(ticks)]
+    scale_link = [link(1 + ticks + t, scale.at[t], scale.at[t]) for t in range(ticks)]
+    enc_link = [
+        link(1 + 2 * ticks + t, made.at[t, first], enc_out.at[t]) for t in range(ticks)
+    ]
+
+    barrier = pltpu.get_barrier_semaphore()
+
+    def greet(segment, row):
+        pl.semaphore_signal(
+            barrier, inc=1, device_id={"segment": segment, "rows": row}, device_id_type=MESH
+        )
+
+    greet(s, 1 - r)
+
+    @pl.when(is_enc & (s > 0))
+    def _():
+        greet(s - 1, 1)
+
+    @pl.when(is_enc & (s < last))
+    def _():
+        greet(s + 1, 1)
+
+    @pl.when(is_dec & (s > 0))
+    def _():
+        greet(s - 1, 0)
+
+    @pl.when(is_dec & (s < last))
+    def _():
+        greet(s + 1, 0)
+
+    within = (s > 0) & (s < last)
+
+    @pl.when(within)
+    def _():
+        pl.semaphore_wait(barrier, 3)
+
+    @pl.when(jnp.logical_not(within))
+    def _():
+        pl.semaphore_wait(barrier, 2 if segments > 1 else 1)
+
+    def spread(source):
+        value = source.reshape(cells, channels).astype(jnp.float32)
+        column = lax.broadcasted_iota(jnp.int32, (cells, channels), 0) % width
+        left = jnp.where(column == 0, 0.0, pltpu.roll(value, 1, 0))
+        right = jnp.where(column == width - 1, 0.0, pltpu.roll(value, cells - 1, 0))
+        body = pl.ds(width, cells)
+        columns[body, 0:channels] = left.astype(jnp.bfloat16)
+        columns[body, channels : 2 * channels] = source.reshape(cells, channels)
+        columns[body, 2 * channels :] = right.astype(jnp.bfloat16)
+
+    def convolve(weights):
+        def tap(d, carry):
+            start = pl.multiple_of(d * width, width)
+            total[...] += jnp.dot(
+                columns[pl.ds(start, cells), :],
+                weights[d].reshape(3 * channels, channels),
+                preferred_element_type=jnp.float32,
+            )
+            return carry
+
+        total[...] = jnp.zeros_like(total)
+        lax.fori_loop(0, taps, tap, 0)
+
+    def skip_part(t, source):
+        spread(source)
+        convolve(skip_kernel)
+        found = total[...]
+        top = jnp.maximum(jnp.max(jnp.abs(found), axis=(0, 1), keepdims=True), 1e-25)
+        scaled = found * (TOP / top)
+        power = scaled * scaled
+        power = power * power
+        power = power * power
+        partial[t] = jnp.where(scaled < 0.0, -power, power).astype(SENT)
+        scale[t] = jnp.broadcast_to(top * (1.0 / TOP), scale.shape[1:])
+        partial_link[t].start()
+        scale_link[t].start()
+
+    def layer(t, value):
+        result = value / (1.0 + jnp.exp(-value))
+        made[t] = result.astype(jnp.bfloat16).reshape(rows, width, channels)
+
+    edge = jnp.zeros((width, 3 * channels), jnp.bfloat16)
+    columns[0:width] = edge
+    columns[width + cells :] = edge
+
+    fresh = [
+        (t, e, segments - (t - e + 1) // 2)
+        for t in range(ticks)
+        for e in range(t)
+        if (t - e) % 2 == 1 and segments >= (t - e + 1) // 2
+    ]
+
+    @pl.when(is_dec)
+    def _():
+        early = ticks // 2
+        for t in range(early):
+            skip_link[t].start()
+        input_link.start()
+        for d in range(taps):
+            weight_link[d].start()
+
+        @pl.when(s == 0)
+        def _():
+            for t in range(ticks - 1):
+                arrival_link[t].start()
+
+        for t in range(early, ticks):
+            skip_link[t].start()
+        mine = local(0, dec_in, held.at[0, first])
+        weights = local(1, dec_w, kernel)
+        mine.start()
+        weights.start()
+        mine.wait()
+        weights.wait()
+        back_input.wait_recv()
+        outs = []
+        for t in range(ticks):
+            if t > 0:
+                relay(t - 1, s, 0).wait_recv()
+            spread(held[t])
+            convolve(kernel)
+            scale_link[t].wait_recv()
+            partial_link[t].wait_recv()
+            power = partial[t].astype(jnp.float32)
+            root = jnp.sqrt(jnp.sqrt(jnp.sqrt(jnp.abs(power))))
+            value = jnp.where(power < 0.0, -root, root) * scale[t, 0:1, 0:1]
+            layer(t, total[...] + value + dec_b[...])
+            if t + 1 < ticks:
+
+                @pl.when(s > 0)
+                def _():
+                    relay(t, s - 1, 0).start()
+
+            dec_link[t].start()
+            keep = local(2 + t, made.at[t, first], dec_out.at[t])
+            keep.start()
+            outs.append(keep)
+        for keep in outs:
+            keep.wait()
+        for t in range(ticks):
+            skip_link[t].wait_send()
+            dec_link[t].wait_send()
+            enc_link[t].wait_recv()
+        input_link.wait_send()
+        for d in range(taps):
+            weight_link[d].wait_send()
+
+        @pl.when(s == 0)
+        def _():
+            for t in range(ticks - 1):
+                arrival_link[t].wait_send()
+
+        @pl.when(s > 0)
+        def _():
+            for t in range(ticks - 1):
+                relay(t, s - 1, 0).wait_send()
+
+    @pl.when(is_enc)
+    def _():
+        back_input.start()
+        own_skips = local(0, skips, skip_full.at[:, final])
+        skip_weights = local(1, dec_w, skip_kernel)
+        mine = local(2, enc_in, held.at[0, final])
+        weights = local(3, enc_w, kernel.at[:, :, pl.ds(part, part)])
+        for copy in (skip_weights, own_skips, mine, weights):
+            copy.start()
+        entering = [local(4 + t, arrivals.at[t], held.at[t + 1, final]) for t in range(ticks - 1)]
+
+        @pl.when(s == 0)
+        def _():
+            for copy in entering:
+                copy.start()
+
+        for copy in (skip_weights, own_skips, mine, weights):
+            copy.wait()
+
+        def buffered(t):
+            skip_link[t].wait_recv()
+            usual = True
+            for tick, _, segment in fresh:
+                if tick == t:
+                    usual = jnp.logical_and(usual, s != segment)
+            if usual is True:
+                skip_part(t, skip_full[t])
+            else:
+
+                @pl.when(usual)
+                def _():
+                    skip_part(t, skip_full[t])
+
+        early = ticks // 2
+        for t in range(early):
+            buffered(t)
+        input_link.wait_recv()
+        for d in range(taps):
+            weight_link[d].wait_recv()
+        outs = []
+        for t in range(ticks):
+            if t > 0:
+
+                @pl.when(s > 0)
+                def _():
+                    relay(t - 1, s, 1).wait_recv()
+
+                @pl.when(s == 0)
+                def _():
+                    arrival_link[t - 1].wait_recv()
+                    entering[t - 1].wait()
+
+            spread(held[t])
+            convolve(kernel)
+            layer(t, total[...] + enc_b[...])
+            if t + 1 < ticks:
+
+                @pl.when(s < last)
+                def _():
+                    relay(t, s + 1, 1).start()
+
+                @pl.when(s == last)
+                def _():
+                    relay(t, s, 0).start()
+
+            for tick, earlier, segment in fresh:
+                if earlier == t:
+
+                    @pl.when(s == segment)
+                    def _():
+                        skip_part(tick, made[t])
+
+            enc_link[t].start()
+            keep = local(4 + ticks + t, made.at[t, final], enc_out.at[t])
+            keep.start()
+            outs.append(keep)
+            if early + t < ticks:
+                buffered(early + t)
+        for keep in outs:
+            keep.wait()
+        back_input.wait_send()
+        for t in range(ticks):
+            partial_link[t].wait_send()
+            scale_link[t].wait_send()
+            enc_link[t].wait_send()
+            dec_link[t].wait_recv()
+
+        @pl.when(s < last)
+        def _():
+            for t in range(ticks - 1):
+                relay(t, s + 1, 1).wait_send()
+
+        @pl.when(s == last)
+        def _():
+            for t in range(ticks - 1):
+                relay(t, s, 0).wait_send()
+
+
+def owned_shards(
+    encoder_weight,
+    encoder_bias,
+    decoder_weight,
+    decoder_bias,
+    encoder_inputs,
+    decoder_inputs,
+    arrivals,
+    skip_buffer,
+):
+    _, ticks, batch, half, width, channels = skip_buffer.shape
+    taps = encoder_weight.shape[1]
+    rows, cells = 2 * half, 2 * half * width
+    links = 3 * ticks + taps
+    anywhere = pl.BlockSpec(memory_space=pl.ANY)
+    vector = pl.BlockSpec(memory_space=pltpu.VMEM)
+    out = jax.ShapeDtypeStruct((ticks, half, width, channels), jnp.bfloat16)
+    image = (rows, width, channels)
+    encoder_made, decoder_made = pl.pallas_call(
+        functools.partial(relay_kernel, lax.axis_size("segment")),
+        out_shape=(out, out),
+        in_specs=[anywhere, vector, anywhere, vector, anywhere, anywhere, anywhere, anywhere],
+        out_specs=(anywhere, anywhere),
+        scratch_shapes=[
+            pltpu.VMEM((taps, 3, channels, channels), jnp.bfloat16),
+            pltpu.VMEM((taps, 3, channels, channels), jnp.bfloat16),
+            pltpu.VMEM((ticks,) + image, jnp.bfloat16),
+            pltpu.VMEM((ticks,) + image, jnp.bfloat16),
+            pltpu.VMEM((ticks,) + image, jnp.bfloat16),
+            pltpu.VMEM((ticks, cells, channels), SENT),
+            pltpu.VMEM((ticks, 8, 128), jnp.float32),
+            pltpu.VMEM((cells + 2 * width, 3 * channels), jnp.bfloat16),
+            pltpu.VMEM((cells, channels), jnp.float32),
+            pltpu.SemaphoreType.DMA((4 + 2 * ticks,)),
+            pltpu.SemaphoreType.DMA((links,)),
+            pltpu.SemaphoreType.DMA((links,)),
+            pltpu.SemaphoreType.DMA((ticks,)),
+            pltpu.SemaphoreType.DMA((ticks,)),
+        ],
+        compiler_params=pltpu.CompilerParams(
+            collective_id=0, has_side_effects=True, vmem_limit_bytes=40 * 1024 * 1024
+        ),
+    )(
+        encoder_weight[0],
+        encoder_bias,
+        decoder_weight[0],
+        decoder_bias,
+        encoder_inputs[0, 0],
+        decoder_inputs[0, 0],
+        arrivals[:, 0],
+        skip_buffer[0, :, 0],
+    )
+    return encoder_made[None, :, None], decoder_made[None, :, None]
+
+
+def gathered_shards(
     encoder_weight,
     encoder_bias,
     decoder_weight,
@@ -148,7 +544,7 @@
 
 def solution(mesh):
     return jax.shard_map(
-        shards,
+        owned_shards if mesh.shape["rows"] == 2 else gathered_shards,
         mesh=mesh,
         in_specs=(
             P("segment", None, None, "rows", None),

time: 227 us -> 94 us (0.41)
  the two profiles are of different devices: /device:TPU:7 before, /device:TPU:31 now
where the time goes in v1:
time: 94 us; the launch traced here: 93.6 us
  Pallas kernels  83 us (88%)
  local copies, waits for them, and re-layouts  9.95 us (11%)
    pallas_call x1, Pallas kernels, owned_shards(): pl.pallas_call(functools.partial(relay_kernel, lax.axis_size('segment')),...  83 us
    unnamed x18, local copies, waits for them, and re-layouts  9.95 us

profile of v1, /device:TPU:31, one launch (start us, length us, event | category | flops | bytes accessed | tf_op | source)
XLA Modules:
  0.0 93.6 jit_solution(2935495526594536674)
XLA Ops:
  0.6 0.0 copy-start
  0.6 1.7 %copy-done = bf16[1,3,3,384,384]{4,3,2,1,0:T(8,128)(2,1)S(1)} copy-done((bf16[1,3,3,384,384]{4,3,2,1,0:T(8,128)(2,1)S(1)}, bf16[1,3,3,384,384]{4,3,2,1,0:T(8,128)(2,1)}, u32[]{:S(2)}) %copy-start) | copy-done | bytes 2654232
  2.4 0.0 copy-start.1
  2.4 1.3 %copy-done.1 = bf16[1,3,3,192,384]{4,3,2,1,0:T(8,128)(2,1)S(1)} copy-done((bf16[1,3,3,192,384]{4,3,2,1,0:T(8,128)(2,1)S(1)}, bf16[1,3,3,192,384]{4,3,2,1,0:T(8,128)(2,1)}, u32[]{:S(2)}) %copy-start.1) | copy-done | bytes 1327128
  3.7 0.0 copy-start.2
  3.7 1.1 %copy-done.2 = bf16[1,4,1,3,64,384]{5,4,3,2,1,0:T(8,128)(2,1)S(1)} copy-done((bf16[1,4,1,3,64,384]{5,4,3,2,1,0:T(8,128)(2,1)S(1)}, bf16[1,4,1,3,64,384]{5,4,3,2,1,0:T(8,128)(2,1)}, u32[]{:S(2)}) %copy-start.2) | copy-done | bytes 589848
  4.8 0.0 copy-start.3
  4.8 1.0 %copy-done.3 = bf16[3,1,3,64,384]{4,3,2,1,0:T(8,128)(2,1)S(1)} copy-done((bf16[3,1,3,64,384]{4,3,2,1,0:T(8,128)(2,1)S(1)}, bf16[3,1,3,64,384]{4,3,2,1,0:T(8,128)(2,1)}, u32[]{:S(2)}) %copy-start.3) | copy-done | bytes 442392
  5.8 0.0 copy-start.4
  5.8 0.9 copy-done.4
  6.7 0.0 copy-start.5
  6.7 0.9 copy-done.5
  7.6 0.0 copy-start.6
  7.6 0.7 copy-done.6
  8.3 0.0 copy-start.7
  8.3 0.7 copy-done.7
  9.0 83.0 %shard_map.95 = (bf16[4,3,64,384]{3,2,1,0:T(8,128)(2,1)S(1)}, bf16[4,3,64,384]{3,2,1,0:T(8,128)(2,1)S(1)}) custom-call(bf16[3,3,192,384]{3,2,1,0:T(8,128)(2,1)S(1)} %bitcast.13, f32[1,384]{1,0:T(1,128)S(1)} %copy-done.6, bf16[3,3,384,384]{3,2,1,0:T(8,128)(2,1)S(1)} %bitcast.12, f32[1,384]{1,0:T(1,128)S(1)} %copy-done.7, bf16[3,64,384]{2,1,0:T(8,128)(2,1)S(1)} %bitcast.18, ...), custom_call_target="tpu_custom_call" | custom-call | tf_op jit(solution)/shard_map/pallas_call | solution.py:414
  92.0 0.8 copy.14
  92.8 0.8 copy.15
Async XLA Ops:
  0.6 1.8 %copy-start = (bf16[1,3,3,384,384]{4,3,2,1,0:T(8,128)(2,1)S(1)}, bf16[1,3,3,384,384]{4,3,2,1,0:T(8,128)(2,1)}, u32[]{:S(2)}) copy-start(bf16[1,3,3,384,384]{4,3,2,1,0:T(8,128)(2,1)} %param.10) | copy-start | bytes 7962628
  2.4 1.3 %copy-start.1 = (bf16[1,3,3,192,384]{4,3,2,1,0:T(8,128)(2,1)S(1)}, bf16[1,3,3,192,384]{4,3,2,1,0:T(8,128)(2,1)}, u32[]{:S(2)}) copy-start(bf16[1,3,3,192,384]{4,3,2,1,0:T(8,128)(2,1)} %param.8) | copy-start | bytes 3981316
  3.7 1.1 %copy-start.2 = (bf16[1,4,1,3,64,384]{5,4,3,2,1,0:T(8,128)(2,1)S(1)}, bf16[1,4,1,3,64,384]{5,4,3,2,1,0:T(8,128)(2,1)}, u32[]{:S(2)}) copy-start(bf16[1,4,1,3,64,384]{5,4,3,2,1,0:T(8,128)(2,1)} %param.15) | copy-start | bytes 1769476
  4.8 1.0 %copy-start.3 = (bf16[3,1,3,64,384]{4,3,2,1,0:T(8,128)(2,1)S(1)}, bf16[3,1,3,64,384]{4,3,2,1,0:T(8,128)(2,1)}, u32[]{:S(2)}) copy-start(bf16[3,1,3,64,384]{4,3,2,1,0:T(8,128)(2,1)} %param.14) | copy-start | bytes 1327108
  5.8 0.9 copy-start.4
  6.7 0.9 copy-start.5
  7.6 0.7 copy-start.6
  8.3 0.7 copy-start.7

commit v2 on v0

--- a/solution.py
+++ b/solution.py
@@ -1,6 +1,10 @@
+import functools
+
 import jax
 import jax.numpy as jnp
 from jax import lax
+from jax.experimental import pallas as pl
+from jax.experimental.pallas import tpu as pltpu
 from jax.sharding import PartitionSpec as P
 
 NUMBERS = ("NHWC", "HWIO", "NHWC")
@@ -52,7 +56,570 @@
     return source[:, excess : source.shape[1] - excess]
 
 
-def shards(
+MESH = pl.DeviceIdType.MESH
+SENT = jnp.bfloat16
+TOP = 32768.0
+
+
+def coded(found):
+    top = jnp.maximum(jnp.max(jnp.abs(found), axis=(0, 1), keepdims=True), 1e-25)
+    scaled = found * (TOP / top)
+    power = scaled * scaled
+    power = power * power
+    power = power * power
+    return jnp.where(scaled < 0.0, -power, power).astype(SENT), top * (1.0 / TOP)
+
+
+def decoded(code, scale):
+    power = code.astype(jnp.float32)
+    root = jnp.sqrt(jnp.sqrt(jnp.sqrt(jnp.abs(power))))
+    return jnp.where(power < 0.0, -root, root) * scale
+
+
+def low_lanes(shape, part):
+    return lax.broadcasted_iota(jnp.int32, shape, 1) < part
+
+
+def packed(value, side):
+    count, part = value.shape[0] // 2, value.shape[1] // 2
+    upper, lower = value[:count], value[count:]
+    left = jnp.where(side == 0, upper, pltpu.roll(upper, part, 1))
+    right = jnp.where(side == 0, pltpu.roll(lower, part, 1), lower)
+    return jnp.where(low_lanes(upper.shape, part), left, right)
+
+
+def unpacked(value, side):
+    part = value.shape[1] // 2
+    turned = pltpu.roll(value, part, 1)
+    return jnp.where(side == 0, value, turned), jnp.where(side == 0, turned, value)
+
+
+def silu(value):
+    return value / (1.0 + jnp.exp(-value))
+
+
+def relay_kernel(
+    segments,
+    enc_w,
+    enc_b,
+    dec_w,
+    dec_b,
+    enc_in,
+    dec_in,
+    arrivals,
+    skips,
+    enc_out,
+    dec_out,
+    wide,
+    narrow,
+    bias,
+    held,
+    made,
+    skip_full,
+    partial,
+    scale,
+    own_in,
+    cut_send,
+    cut_recv,
+    sum_send,
+    sum_recv,
+    sum_scale_send,
+    sum_scale_recv,
+    enc_held,
+    enc_made,
+    enc_other,
+    out_send,
+    out_recv,
+    enc_final,
+    columns,
+    total,
+    mine,
+    flat,
+    local_sem,
+    link_send,
+    link_recv,
+    relay_send,
+    relay_recv,
+):
+    s = lax.axis_index("segment")
+    r = lax.axis_index("rows")
+    ticks, half, width, channels = skips.shape
+    rows = 2 * half
+    cells = rows * width
+    own = half * width
+    taps = enc_w.shape[0]
+    part = enc_w.shape[2]
+    slot = narrow.shape[2]
+    last = segments - 1
+    is_enc = r == 1
+    is_dec = r == 0
+    counter = [0]
+
+    def link(src, dst):
+        number = counter[0]
+        counter[0] = number + 1
+        return pltpu.make_async_remote_copy(
+            src_ref=src,
+            dst_ref=dst,
+            send_sem=link_send.at[number],
+            recv_sem=link_recv.at[number],
+            device_id={"segment": s, "rows": 1 - r},
+            device_id_type=MESH,
+        )
+
+    def relay(number, src, dst, segment):
+        return pltpu.make_async_remote_copy(
+            src_ref=src,
+            dst_ref=dst,
+            send_sem=relay_send.at[number],
+            recv_sem=relay_recv.at[number],
+            device_id={"segment": segment, "rows": r},
+            device_id_type=MESH,
+        )
+
+    def local(src, dst):
+        number = counter[0]
+        counter[0] = number + 1
+        return pltpu.make_async_copy(src, dst, local_sem.at[number])
+
+    def enc_relay(t):
+        return relay(t, enc_made.at[t], enc_held.at[t + 1], s + 1)
+
+    def dec_relay(t):
+        return relay(ticks + t, made.at[t], held.at[t + 1], s - 1)
+
+    first, final = pl.ds(0, half), pl.ds(half, half)
+
+    cut_link = [link(cut_send.at[t], cut_recv.at[t]) for t in range(ticks)]
+    sum_link = [link(sum_send.at[t], sum_recv.at[t]) for t in range(ticks)]
+    sum_scale_link = [link(sum_scale_send.at[t], sum_scale_recv.at[t]) for t in range(ticks)]
+    out_link = [link(out_send.at[t], out_recv.at[t]) for t in range(ticks)]
+    whole_link = [link(enc_made.at[t], enc_other.at[t]) for t in range(ticks - 1)]
+    skip_link = [link(skips.at[t], skip_full.at[t, first]) for t in range(ticks)]
+    dec_link = [link(made.at[t, final], dec_out.at[t]) for t in range(ticks)]
+    back_input = link(dec_in, held.at[0, final])
+    partial_link = [link(partial.at[t], partial.at[t]) for t in range(ticks)]
+    scale_link = [link(scale.at[t], scale.at[t]) for t in range(ticks)]
+
+    counter[0] = 0
+    enc_load = local(enc_in, own_in.at[0])
+    enter_load = [local(arrivals.at[t], own_in.at[t + 1]) for t in range(ticks - 1)]
+    narrow_load = local(enc_w, narrow.at[:, :, pl.ds(0, part)])
+    wide_load = local(dec_w, wide)
+    enc_b_load = local(enc_b, bias.at[pl.ds(0, 1)])
+    dec_b_load = local(dec_b, bias.at[pl.ds(8, 1)])
+    dec_load = local(dec_in, held.at[0, first])
+    skip_load = local(skips, skip_full.at[:, final])
+    enc_store = [local(enc_final.at[t], enc_out.at[t]) for t in range(ticks)]
+    dec_store = [local(made.at[t, first], dec_out.at[t]) for t in range(ticks)]
+
+    for copy in (enc_load, narrow_load, enc_b_load, dec_b_load, wide_load):
+        copy.start()
+
+    @pl.when(is_dec)
+    def _():
+        dec_load.start()
+
+    @pl.when(is_enc)
+    def _():
+        skip_load.start()
+
+    @pl.when(s == 0)
+    def _():
+        for copy in enter_load:
+            copy.start()
+
+    barrier = pltpu.get_barrier_semaphore()
+
+    def greet(segment, row):
+        pl.semaphore_signal(
+            barrier, inc=1, device_id={"segment": segment, "rows": row}, device_id_type=MESH
+        )
+
+    greet(s, 1 - r)
+
+    @pl.when(s > 0)
+    def _():
+        greet(s - 1, r)
+
+    @pl.when(s < last)
+    def _():
+        greet(s + 1, r)
+
+    within = (s > 0) & (s < last)
+
+    @pl.when(within)
+    def _():
+        pl.semaphore_wait(barrier, 3)
+
+    @pl.when(jnp.logical_not(within))
+    def _():
+        pl.semaphore_wait(barrier, 2 if segments > 1 else 1)
+
+    body = pl.ds(width, cells)
+
+    def spread(value, span):
+        column = lax.broadcasted_iota(jnp.int32, value.shape, 0) % width
+        left = jnp.where(column == 0, 0.0, pltpu.roll(value, 1, 0))
+        right = jnp.where(column == width - 1, 0.0, pltpu.roll(value, cells - 1, 0))
+        columns[body, 0:span] = left.astype(jnp.bfloat16)
+        columns[body, span : 2 * span] = value.astype(jnp.bfloat16)
+        columns[body, 2 * span : 3 * span] = right.astype(jnp.bfloat16)
+
+    def convolve(weights, span):
+        def tap(d, carry):
+            start = pl.multiple_of(d * width, width)
+            total[...] += jnp.dot(
+                columns[pl.ds(start, cells), 0 : 3 * span],
+                weights[d].reshape(3 * span, channels),
+                preferred_element_type=jnp.float32,
+            )
+            return carry
+
+        total[...] = jnp.zeros_like(total)
+        lax.fori_loop(0, taps, tap, 0)
+
+    def skip_part(t):
+        convolve(wide, channels)
+        code, unit = coded(total[...])
+        partial[t] = code
+        scale[t] = jnp.broadcast_to(unit, scale.shape[1:])
+        partial_link[t].start()
+        scale_link[t].start()
+
+    def image(ref):
+        return ref[...].reshape(-1, channels).astype(jnp.float32)
+
+    def whole(t):
+        here = unpacked(enc_made[t].astype(jnp.float32), r)
+        there = unpacked(enc_other[t].astype(jnp.float32), 1 - r)
+        keep = low_lanes((own, channels), part) == (r == 0)
+        for number in range(2):
+            flat[pl.ds(number * own, own)] = jnp.where(keep, here[number], there[number])
+
+    def cut(t):
+        cut_send[t] = packed(image(own_in.at[t]), 1 - r).astype(jnp.bfloat16)
+        cut_link[t].start()
+
+    def enter(t):
+        value = image(own_in.at[t])
+        here = jnp.where(r == 0, value, pltpu.roll(value, part, 1))
+        there = jnp.concatenate(unpacked(cut_recv[t].astype(jnp.float32), 0), axis=0)
+        flat[pl.ds(0, own)] = jnp.where(r == 0, here, there)
+        flat[pl.ds(own, own)] = jnp.where(r == 0, there, here)
+
+    def enc_sums(t):
+        if t == 0:
+            cut_link[0].wait_recv()
+            enter(0)
+        else:
+
+            @pl.when(s == 0)
+            def _():
+                enter_wait(t)
+                enter(t)
+
+            @pl.when(s > 0)
+            def _():
+                enc_relay(t - 1).wait_recv()
+                upper, lower = unpacked(enc_held[t].astype(jnp.float32), 0)
+                flat[pl.ds(0, own)] = upper
+                flat[pl.ds(own, own)] = lower
+
+        value = flat[:, 0:slot]
+        spread(jnp.where(low_lanes(value.shape, part), value, 0.0), slot)
+        convolve(narrow, slot)
+        sums = total[...]
+        code, unit = coded(packed(sums, 1 - r))
+        sum_send[t] = code
+        sum_scale_send[t] = jnp.broadcast_to(unit, sum_scale_send.shape[1:])
+        sum_link[t].start()
+        sum_scale_link[t].start()
+        mine[...] = packed(sums, r)
+
+    def enter_wait(t):
+        cut_link[t].wait_recv()
+
+    def enc_finish(t):
+        line = jnp.broadcast_to(bias[0:1], (8, channels))
+        turned = pltpu.roll(line, part, 1)
+        low = low_lanes(line.shape, part)
+        line = jnp.where(low == (r == 0), line, turned)[0:1]
+        sum_scale_link[t].wait_recv()
+        sum_link[t].wait_recv()
+        value = mine[...] + decoded(sum_recv[t], sum_scale_recv[t, 0:1, 0:1]) + line
+        result = silu(value).astype(jnp.bfloat16)
+        enc_made[t] = result
+        if t + 1 < ticks:
+
+            @pl.when(s < last)
+            def _():
+                enc_relay(t).start()
+
+            @pl.when(s == last)
+            def _():
+                whole_link[t].start()
+
+            for segment in sorted({seg for _, e, seg in fresh if e == t and seg < last}):
+
+                @pl.when(is_dec & (s == segment))
+                def _():
+                    whole_link[t].start()
+
+        out_send[t] = packed(result.astype(jnp.float32), 1 - r).astype(jnp.bfloat16)
+        out_link[t].start()
+
+    def enc_store_rows(t):
+        out_link[t].wait_recv()
+        value = enc_made[t].astype(jnp.float32)
+        upper = low_lanes(value.shape, part)
+        there = jnp.concatenate(unpacked(out_recv[t].astype(jnp.float32), 1 - r), axis=0)
+        enc_final[t] = (
+            jnp.where(upper == (r == 0), value, there)
+            .astype(jnp.bfloat16)
+            .reshape(half, width, channels)
+        )
+        enc_store[t].start()
+
+    fresh = [
+        (t, e, segments - (t - e + 1) // 2)
+        for t in range(ticks)
+        for e in range(t)
+        if (t - e) % 2 == 1 and segments >= (t - e + 1) // 2
+    ]
+
+    enc_load.wait()
+    cut(0)
+
+    @pl.when(is_dec)
+    def _():
+        for t in range(min(2, ticks)):
+            skip_link[t].start()
+
+    @pl.when(is_enc)
+    def _():
+        back_input.start()
+
+    @pl.when(s == 0)
+    def _():
+        for copy in enter_load:
+            copy.wait()
+        for t in range(1, ticks):
+            cut(t)
+
+    edge = jnp.zeros((width, 3 * channels), jnp.bfloat16)
+    columns[0:width] = edge
+    columns[width + cells :] = edge
+    for copy in (narrow_load, enc_b_load, dec_b_load, wide_load):
+        copy.wait()
+    if slot > part:
+        narrow[:, :, part:] = jnp.zeros((taps, 3, slot - part, channels), jnp.bfloat16)
+
+    @pl.when(is_dec)
+    def _():
+        dec_load.wait()
+
+        def layer(t):
+            if t == 0:
+                back_input.wait_recv()
+            else:
+
+                @pl.when(s < last)
+                def _():
+                    dec_relay(t - 1).wait_recv()
+
+                @pl.when(s == last)
+                def _():
+                    whole_link[t - 1].wait_recv()
+                    whole(t - 1)
+                    held[t] = flat[...].astype(jnp.bfloat16).reshape(rows, width, channels)
+
+            spread(image(held.at[t]), channels)
+            convolve(wide, channels)
+            scale_link[t].wait_recv()
+            partial_link[t].wait_recv()
+            value = total[...] + decoded(partial[t], scale[t, 0:1, 0:1]) + bias[8:9]
+            made[t] = silu(value).astype(jnp.bfloat16).reshape(rows, width, channels)
+            if t + 1 < ticks:
+
+                @pl.when(s > 0)
+                def _():
+                    dec_relay(t).start()
+
+            dec_link[t].start()
+            dec_store[t].start()
+
+        for t in range(ticks):
+            enc_sums(t)
+            if t + 2 < ticks:
+                skip_link[t + 2].start()
+            if t > 0:
+                layer(t - 1)
+            enc_finish(t)
+            if t > 0:
+                enc_store_rows(t - 1)
+        layer(ticks - 1)
+        enc_store_rows(ticks - 1)
+        for t in range(ticks):
+            skip_link[t].wait_send()
+            dec_link[t].wait_send()
+            dec_store[t].wait()
+
+        @pl.when(s > 0)
+        def _():
+            for t in range(ticks - 1):
+                dec_relay(t).wait_send()
+
+        for earlier, segment in sorted({(e, seg) for _, e, seg in fresh if seg < last}):
+
+            @pl.when(s == segment)
+            def _():
+                whole_link[earlier].wait_send()
+
+    @pl.when(is_enc)
+    def _():
+        skip_load.wait()
+
+        def buffered(t):
+            skip_link[t].wait_recv()
+            usual = s >= 0
+            for tick, _, segment in fresh:
+                if tick == t:
+                    usual = jnp.logical_and(usual, s != segment)
+
+            @pl.when(usual)
+            def _():
+                spread(image(skip_full.at[t]), channels)
+                skip_part(t)
+
+        for t in range(ticks):
+            enc_sums(t)
+            buffered(t)
+            enc_finish(t)
+            for tick, earlier, segment in fresh:
+                if earlier == t:
+
+                    @pl.when(s == segment)
+                    def _():
+                        if tick == earlier + 1 or segment < last:
+                            whole_link[t].wait_recv()
+                        whole(t)
+                        spread(flat[...], channels)
+                        skip_part(tick)
+
+            if t > 0:
+                enc_store_rows(t - 1)
+        enc_store_rows(ticks - 1)
+        back_input.wait_send()
+        for t in range(ticks):
+            partial_link[t].wait_send()
+            scale_link[t].wait_send()
+            dec_link[t].wait_recv()
+
+    cut_link[0].wait_send()
+    for t in range(ticks):
+        sum_link[t].wait_send()
+        sum_scale_link[t].wait_send()
+        out_link[t].wait_send()
+        enc_store[t].wait()
+
+    @pl.when(s == 0)
+    def _():
+        for t in range(1, ticks):
+            cut_link[t].wait_send()
+
+    @pl.when(s < last)
+    def _():
+        for t in range(ticks - 1):
+            enc_relay(t).wait_send()
+
+    @pl.when(s == last)
+    def _():
+        for t in range(ticks - 1):
+            whole_link[t].wait_send()
+
+
+def owned_shards(
+    encoder_weight,
+    encoder_bias,
+    decoder_weight,
+    decoder_bias,
+    encoder_inputs,
+    decoder_inputs,
+    arrivals,
+    skip_buffer,
+):
+    _, ticks, batch, half, width, channels = skip_buffer.shape
+    taps, part = encoder_weight.shape[1], encoder_weight.shape[3]
+    rows, own = 2 * half, half * width
+    cells = 2 * own
+    links = 9 * ticks + 9 * ticks
+    slot = -(-part // 128) * 128
+    anywhere = pl.BlockSpec(memory_space=pl.ANY)
+    main = pl.BlockSpec(memory_space=pltpu.HBM)
+    out = jax.ShapeDtypeStruct((ticks, half, width, channels), jnp.bfloat16)
+    image = (ticks, rows, width, channels)
+
+    def brief(*shape):
+        return pltpu.VMEM(shape, jnp.bfloat16)
+
+    def full(*shape):
+        return pltpu.VMEM(shape, jnp.float32)
+
+    encoder_made, decoder_made = pl.pallas_call(
+        functools.partial(relay_kernel, lax.axis_size("segment")),
+        out_shape=(out, out),
+        in_specs=[main] * 8,
+        out_specs=(anywhere, anywhere),
+        scratch_shapes=[
+            brief(taps, 3, channels, channels),
+            brief(taps, 3, slot, channels),
+            full(16, channels),
+            brief(*image),
+            brief(*image),
+            brief(*image),
+            brief(ticks, cells, channels),
+            full(ticks, 8, 128),
+            brief(ticks, half, width, channels),
+            brief(ticks, own // 2, channels),
+            brief(ticks, own // 2, channels),
+            brief(ticks, own, channels),
+            brief(ticks, own, channels),
+            full(ticks, 8, 128),
+            full(ticks, 8, 128),
+            brief(ticks, own, channels),
+            brief(ticks, own, channels),
+            brief(ticks, own, channels),
+            brief(ticks, own // 2, channels),
+            brief(ticks, own // 2, channels),
+            brief(ticks, half, width, channels),
+            brief(cells + 2 * width, 3 * channels),
+            full(cells, channels),
+            full(own, channels),
+            full(cells, channels),
+            pltpu.SemaphoreType.DMA((10 + 4 * ticks,)),
+            pltpu.SemaphoreType.DMA((links,)),
+            pltpu.SemaphoreType.DMA((links,)),
+            pltpu.SemaphoreType.DMA((2 * ticks,)),
+            pltpu.SemaphoreType.DMA((2 * ticks,)),
+        ],
+        compiler_params=pltpu.CompilerParams(
+            collective_id=0, has_side_effects=True, vmem_limit_bytes=40 * 1024 * 1024
+        ),
+    )(
+        encoder_weight[0],
+        encoder_bias,
+        decoder_weight[0],
+        decoder_bias,
+        encoder_inputs[0, 0],
+        decoder_inputs[0, 0],
+        arrivals[:, 0],
+        skip_buffer[0, :, 0],
+    )
+    return encoder_made[None, :, None], decoder_made[None, :, None]
+
+
+def gathered_shards(
     encoder_weight,
     encoder_bias,
     decoder_weight,
@@ -148,7 +715,7 @@
 
 def solution(mesh):
     return jax.shard_map(
-        shards,
+        owned_shards if mesh.shape["rows"] == 2 else gathered_shards,
         mesh=mesh,
         in_specs=(
             P("segment", None, None, "rows", None),

time: 227 us -> 82.2 us (0.36)
  the two profiles are of different devices: /device:TPU:7 before, /device:TPU:31 now
where the time goes in v2:
time: 82.2 us; the launch traced here: 81.8 us
  Pallas kernels  71.2 us (87%)
  local copies, waits for them, and re-layouts  9.95 us (12%)
    pallas_call x1, Pallas kernels, owned_shards(): pl.pallas_call(functools.partial(relay_kernel, lax.axis_size('segment')),...  71.2 us
    unnamed x18, local copies, waits for them, and re-layouts  9.95 us

profile of v2, /device:TPU:31, one launch (start us, length us, event | category | flops | bytes accessed | tf_op | source)
XLA Modules:
  0.0 81.8 jit_solution(8657008955008730271)
XLA Ops:
  0.6 0.0 copy-start
  0.6 1.7 %copy-done = bf16[1,3,3,384,384]{4,3,2,1,0:T(8,128)(2,1)S(1)} copy-done((bf16[1,3,3,384,384]{4,3,2,1,0:T(8,128)(2,1)S(1)}, bf16[1,3,3,384,384]{4,3,2,1,0:T(8,128)(2,1)}, u32[]{:S(2)}) %copy-start) | copy-done | bytes 2654232
  2.4 0.0 copy-start.1
  2.4 1.3 %copy-done.1 = bf16[1,3,3,192,384]{4,3,2,1,0:T(8,128)(2,1)S(1)} copy-done((bf16[1,3,3,192,384]{4,3,2,1,0:T(8,128)(2,1)S(1)}, bf16[1,3,3,192,384]{4,3,2,1,0:T(8,128)(2,1)}, u32[]{:S(2)}) %copy-start.1) | copy-done | bytes 1327128
  3.7 0.0 copy-start.2
  3.7 1.1 %copy-done.2 = bf16[1,4,1,3,64,384]{5,4,3,2,1,0:T(8,128)(2,1)S(1)} copy-done((bf16[1,4,1,3,64,384]{5,4,3,2,1,0:T(8,128)(2,1)S(1)}, bf16[1,4,1,3,64,384]{5,4,3,2,1,0:T(8,128)(2,1)}, u32[]{:S(2)}) %copy-start.2) | copy-done | bytes 589848
  4.8 0.0 copy-start.3
  4.8 1.0 %copy-done.3 = bf16[3,1,3,64,384]{4,3,2,1,0:T(8,128)(2,1)S(1)} copy-done((bf16[3,1,3,64,384]{4,3,2,1,0:T(8,128)(2,1)S(1)}, bf16[3,1,3,64,384]{4,3,2,1,0:T(8,128)(2,1)}, u32[]{:S(2)}) %copy-start.3) | copy-done | bytes 442392
  5.8 0.0 copy-start.4
  5.8 0.9 %copy-done.4 = bf16[1,1,3,64,384]{4,3,2,1,0:T(8,128)(2,1)S(1)} copy-done((bf16[1,1,3,64,384]{4,3,2,1,0:T(8,128)(2,1)S(1)}, bf16[1,1,3,64,384]{4,3,2,1,0:T(8,128)(2,1)}, u32[]{:S(2)}) %copy-start.4) | copy-done | bytes 147480
  6.7 0.0 copy-start.5
  6.7 0.9 %copy-done.5 = bf16[1,1,3,64,384]{4,3,2,1,0:T(8,128)(2,1)S(1)} copy-done((bf16[1,1,3,64,384]{4,3,2,1,0:T(8,128)(2,1)S(1)}, bf16[1,1,3,64,384]{4,3,2,1,0:T(8,128)(2,1)}, u32[]{:S(2)}) %copy-start.5) | copy-done | bytes 147480
  7.6 0.0 copy-start.6
  7.6 0.7 copy-done.6
  8.3 0.0 copy-start.7
  8.3 0.7 copy-done.7
  9.0 71.2 %shard_map.95 = (bf16[4,3,64,384]{3,2,1,0:T(8,128)(2,1)S(1)}, bf16[4,3,64,384]{3,2,1,0:T(8,128)(2,1)S(1)}) custom-call(bf16[3,3,192,384]{3,2,1,0:T(8,128)(2,1)S(1)} %bitcast.13, f32[1,384]{1,0:T(1,128)S(1)} %copy-done.6, bf16[3,3,384,384]{3,2,1,0:T(8,128)(2,1)S(1)} %bitcast.12, f32[1,384]{1,0:T(1,128)S(1)} %copy-done.7, bf16[3,64,384]{2,1,0:T(8,128)(2,1)S(1)} %bitcast.18, ...), custom_call_target="tpu_custom_call" | custom-call | tf_op jit(solution)/shard_map/pallas_call | solution.py:569
  80.2 0.8 copy.14
  81.0 0.8 copy.15
Async XLA Ops:
  0.6 1.8 %copy-start = (bf16[1,3,3,384,384]{4,3,2,1,0:T(8,128)(2,1)S(1)}, bf16[1,3,3,384,384]{4,3,2,1,0:T(8,128)(2,1)}, u32[]{:S(2)}) copy-start(bf16[1,3,3,384,384]{4,3,2,1,0:T(8,128)(2,1)} %param.10) | copy-start | bytes 7962628
  2.4 1.3 %copy-start.1 = (bf16[1,3,3,192,384]{4,3,2,1,0:T(8,128)(2,1)S(1)}, bf16[1,3,3,192,384]{4,3,2,1,0:T(8,128)(2,1)}, u32[]{:S(2)}) copy-start(bf16[1,3,3,192,384]{4,3,2,1,0:T(8,128)(2,1)} %param.8) | copy-start | bytes 3981316
  3.7 1.1 %copy-start.2 = (bf16[1,4,1,3,64,384]{5,4,3,2,1,0:T(8,128)(2,1)S(1)}, bf16[1,4,1,3,64,384]{5,4,3,2,1,0:T(8,128)(2,1)}, u32[]{:S(2)}) copy-start(bf16[1,4,1,3,64,384]{5,4,3,2,1,0:T(8,128)(2,1)} %param.15) | copy-start | bytes 1769476
  4.8 1.0 %copy-start.3 = (bf16[3,1,3,64,384]{4,3,2,1,0:T(8,128)(2,1)S(1)}, bf16[3,1,3,64,384]{4,3,2,1,0:T(8,128)(2,1)}, u32[]{:S(2)}) copy-start(bf16[3,1,3,64,384]{4,3,2,1,0:T(8,128)(2,1)} %param.14) | copy-start | bytes 1327108
  5.8 0.9 %copy-start.4 = (bf16[1,1,3,64,384]{4,3,2,1,0:T(8,128)(2,1)S(1)}, bf16[1,1,3,64,384]{4,3,2,1,0:T(8,128)(2,1)}, u32[]{:S(2)}) copy-start(bf16[1,1,3,64,384]{4,3,2,1,0:T(8,128)(2,1)} %param.12) | copy-start | bytes 442372
  6.7 0.9 %copy-start.5 = (bf16[1,1,3,64,384]{4,3,2,1,0:T(8,128)(2,1)S(1)}, bf16[1,1,3,64,384]{4,3,2,1,0:T(8,128)(2,1)}, u32[]{:S(2)}) copy-start(bf16[1,1,3,64,384]{4,3,2,1,0:T(8,128)(2,1)} %param.13) | copy-start | bytes 442372
  7.6 0.7 copy-start.6
  8.3 0.7 copy-start.7

commit v3 on v2

--- a/solution.py
+++ b/solution.py
@@ -604,7 +604,7 @@
             pltpu.SemaphoreType.DMA((2 * ticks,)),
         ],
         compiler_params=pltpu.CompilerParams(
-            collective_id=0, has_side_effects=True, vmem_limit_bytes=40 * 1024 * 1024
+            collective_id=0, has_side_effects=True, vmem_limit_bytes=63 * 1024 * 1024
         ),
     )(
         encoder_weight[0],

time: 82.2 us -> 75.3 us (0.916)
  local copies, waits for them, and re-layouts: 9.95 us -> 3.88 us
    unnamed x18 -> x2, local copies, waits for them, and re-layouts: 9.95 us -> 3.88 us
where the time goes in v3:
time: 75.3 us; the launch traced here: 75.1 us
  Pallas kernels  70.5 us (94%)
  local copies, waits for them, and re-layouts  3.88 us (5%)
    pallas_call x1, Pallas kernels, owned_shards(): pl.pallas_call(functools.partial(relay_kernel, lax.axis_size('segment')),...  70.5 us
    unnamed x2, local copies, waits for them, and re-layouts  3.88 us

profile of v3, /device:TPU:31, one launch (start us, length us, event | category | flops | bytes accessed | tf_op | source)
XLA Modules:
  0.0 75.1 jit_solution(12778128010575218123)
XLA Ops:
  0.6 70.5 %shard_map.95 = (bf16[4,3,64,384]{3,2,1,0:T(8,128)(2,1)}, bf16[4,3,64,384]{3,2,1,0:T(8,128)(2,1)}) custom-call(bf16[3,3,192,384]{3,2,1,0:T(8,128)(2,1)} %bitcast.13, f32[1,384]{1,0:T(1,128)} %enc_b.1, bf16[3,3,384,384]{3,2,1,0:T(8,128)(2,1)} %bitcast.12, f32[1,384]{1,0:T(1,128)} %dec_b.1, bf16[3,64,384]{2,1,0:T(8,128)(2,1)} %bitcast.18, ...), custom_call_target="tpu_custom_call" | custom-call | tf_op jit(solution)/shard_map/pallas_call | solution.py:569
  71.2 1.9 %copy.14 = bf16[1,4,1,3,64,384]{5,4,3,2,1,0:T(8,128)(2,1)} copy(bf16[1,4,1,3,64,384]{5,4,3,2,1,0:T(8,128)(2,1)} %bitcast.15) | data formatting | bytes 1179648
  73.1 1.9 %copy.15 = bf16[1,4,1,3,64,384]{5,4,3,2,1,0:T(8,128)(2,1)} copy(bf16[1,4,1,3,64,384]{5,4,3,2,1,0:T(8,128)(2,1)} %bitcast.14) | data formatting | bytes 1179648
